TPU v7x, 512 devices: a whole 4x8x8 slice. The times are simulated.
512 devices in a mesh: fsdp: 32 (over y, x), ctx: 8 (over z), tp: 2 (over core).
Axes of the slice: x: 4, y: 8, z: 8, core: 2. Of those that a mesh axis runs over, the one named last changes fastest.
Arguments:
- tokens: bfloat16 [1, 4096, 8192], P(None, 'ctx', ('fsdp', 'tp')), may hold values from -6 to 6
- w_in: bfloat16 [8192, 3, 8192], P('ctx', None, ('fsdp', 'tp')), may hold values from -0.0625 to 0.0625
- short_taps: float32 [7, 3, 8192], P(None, None, ('fsdp', 'tp')), may hold values from -2 to 2
- mr_taps: float32 [128, 8192], P(None, ('fsdp', 'tp')), may hold values from -1 to 1
- skip: float32 [8192], P(('fsdp', 'tp')), may hold values from 0.5 to 1.5
- genome_ids: int32 [1, 4096], replicated, may hold values from 0 to 3, never falling along the last dimension, each value on 1 to 2048 neighbouring positions
Outputs:
- gated: bfloat16 [1, 4096, 8192], P(None, 'ctx', ('fsdp', 'tp'))
Inputs may be any that keep to these rules, and one draw needn't show every extreme that they name: `genome_ids`: ids never fall along a sequence; each genome holds 1 to 2048 positions, and one holds exactly 2048.
All inputs are finite; a program needn't handle non-finite values.
Results may differ from a plain program's by a relative error of at most 0.007.
Values may be sent and summed in bfloat16 or wider, within the bound.
No kernel may reach another device: no remote copies, remote signals or barrier semaphores. Data moves between devices by JAX's collectives and lax.ppermute only.
A program may use at most 64 MiB of HBM per device.

v0:
```python
import jax
import jax.numpy as jnp
from jax import lax
from jax.sharding import PartitionSpec as P


def passed_along(value, axis, steps):
    count = lax.axis_size(axis)
    leading, last = (max(0, -steps), min(count, count - steps))
    return lax.ppermute(value, axis, [(source, source + steps) for source in range(leading, last)])


def causal_mix(padded, segment_pad, taps, count):
    reach = taps.shape[0] - 1
    target = segment_pad[:, reach : reach + count]

    def add_lag(offset, total):
        piece = lax.dynamic_slice_in_dim(padded, reach - offset, count, 1).astype(jnp.float32)
        source = lax.dynamic_slice_in_dim(segment_pad, reach - offset, count, 1)
        same = (source == target).astype(jnp.float32)[..., None]
        weight = lax.dynamic_index_in_dim(taps, offset, 0, keepdims=False)
        return total + weight * piece * same

    start = jnp.zeros(padded.shape[:1] + (count,) + padded.shape[2:], jnp.float32)
    return lax.fori_loop(0, reach + 1, add_lag, start)


def body(tokens, w_in, short_taps, mr_taps, skip, genome_ids):
    length = tokens.shape[1]
    channels = short_taps.shape[2]
    short_reach = short_taps.shape[0] - 1
    long_reach = mr_taps.shape[0] - 1
    block = lax.all_gather(tokens, "tp", axis=2, tiled=True)
    panel_all = lax.all_gather(w_in, "ctx", axis=0, tiled=True).reshape(-1, 3 * channels)
    summed = jnp.einsum(
        "bld,dk->blk",
        lax.all_gather(block, "fsdp", axis=2, tiled=True),
        panel_all,
        preferred_element_type=jnp.float32,
    )
    raw = summed.astype(jnp.bfloat16)
    position = lax.axis_index("ctx") * length
    both_reach = long_reach + short_reach
    ids_padded = jnp.pad(genome_ids, ((0, 0), (both_reach, 0)), constant_values=-1)
    segment_long = lax.dynamic_slice_in_dim(
        ids_padded, position + short_reach, length + long_reach, 1
    )
    taps_short = short_taps.reshape(short_taps.shape[0], -1)
    rim_rows = passed_along(raw[:, length - short_reach :, :], "ctx", 1)
    segment_short = lax.dynamic_slice_in_dim(
        ids_padded, position + long_reach, length + short_reach, 1
    )
    featured = causal_mix(jnp.concatenate([rim_rows, raw], 1), segment_short, taps_short, length)
    queries = featured[..., :channels]
    mixed = (featured[..., channels : 2 * channels] * featured[..., 2 * channels :]).astype(
        jnp.bfloat16
    )
    earlier = passed_along(mixed[:, length - long_reach :, :], "ctx", 1)
    mixed_pad = jnp.concatenate([earlier, mixed], 1)
    filtered = causal_mix(mixed_pad, segment_long, mr_taps, length)
    return (queries * (filtered + skip * mixed.astype(jnp.float32))).astype(jnp.bfloat16)


def solution(mesh):
    in_specs = (
        P(None, "ctx", ("fsdp", "tp")),
        P("ctx", None, ("fsdp", "tp")),
        P(None, None, ("fsdp", "tp")),
        P(None, ("fsdp", "tp")),
        P(("fsdp", "tp")),
        P(),
    )
    out_specs = P(None, "ctx", ("fsdp", "tp"))
    return jax.shard_map(body, mesh=mesh, in_specs=in_specs, out_specs=out_specs, check_vma=False)
```

profile of v0, /device:TPU:192, one launch (start us, length us, event | category | flops | bytes accessed | tf_op | source)
XLA Modules:
  0.0 362.7 jit_solution(16559129843898876737)
XLA Ops:
  6.5 2.3 copy.7
  8.9 3.5 all_gather.9
  12.5 0.8 constant_dynamic-slice_fusion.1
  13.3 75.4 %all-gather.5.cloned.1.call-done = bf16[8192,3,128]{0,2,1:T(8,128)(2,1)} async-done(((bf16[1024,3,128]{0,2,1:T(8,128)(2,1)}), bf16[8192,3,128]{0,2,1:T(8,128)(2,1)}) %all-gather.5.cloned.1.call-update) | async-done | bytes 6291472 | tf_op jit(solution)/shard_map/all_gather | solution.py:34
  88.7 111.1 %all-gather.3.cloned.1.call-done = bf16[1,512,8192]{2,1,0:T(8,128)(2,1)} async-done(((bf16[1,512,256]{2,1,0:T(8,128)(2,1)}), bf16[1,512,8192]{2,1,0:T(8,128)(2,1)}) %all-gather.3.cloned.1.call-update) | async-done | bytes 8388624 | tf_op jit(solution)/shard_map/all_gather | solution.py:37
  199.9 9.7 %fusion.6 = bf16[1,512,384]{2,1,0:T(8,128)(2,1)S(1)} fusion(bf16[8192,384]{0,1:T(8,128)(2,1)} %bitcast.25, bf16[1,512,8192]{2,1,0:T(8,128)(2,1)} %all-gather.3.cloned.1.call-done), kind=kOutput, calls=%fused_computation.10 | convolution fusion | flops 3221422080 | bytes 15073280 | tf_op jit(solution)/shard_map/bld,dk->blk/dot_general | solution.py:35
  209.6 4.8 %collective-permute-start = (bf16[1,6,384]{2,1,0:T(8,128)(2,1)S(1)}, bf16[1,6,384]{2,1,0:T(8,128)(2,1)S(1)}, u32[]{:S(2)}, u32[]{:S(2)}) collective-permute-start(bf16[1,6,384]{2,1,0:T(8,128)(2,1)S(1)} %slice.28), channel_id=1, source_target_pairs={{0,2},{2,4},{4,6},{6,8},{8,10},{10,12},{12,14},{1,3},{3,5},{5,7},{... | collective-permute-start | bytes 13832 | tf_op jit(solution)/shard_map/ppermute | solution.py:10
  214.5 1.2 collective-permute-done
  215.8 7.9 %while.32 = (s32[]{:T(128)}, f32[1,512,384]{2,1,0:T(8,128)S(1)}, f32[7,384]{1,0:T(8,128)}, bf16[1,518,384]{2,1,0:T(8,128)(2,1)S(1)}, s32[1,518]{1,0:T(1,128)S(1)...) while((s32[]{:T(128)}, f32[1,512,384]{2,1,0:T(8,128)S(1)}, ...), condition=%wide.region_1.2_spmd.clone, body=%wide.region_0.1_spmd.clone.sunk | while | flops 984071 | bytes 1979049 | solution.py:25
  215.9 0.7 dynamic-slice_reduce_fusion.2
  217.0 0.7 dynamic-slice_reduce_fusion.2
  218.2 0.7 dynamic-slice_reduce_fusion.2
  219.3 0.7 dynamic-slice_reduce_fusion.2
  220.4 0.7 dynamic-slice_reduce_fusion.2
  221.6 0.7 dynamic-slice_reduce_fusion.2
  222.7 0.7 dynamic-slice_reduce_fusion.2
  223.8 5.4 %collective-permute-start.1 = (bf16[1,127,128]{2,1,0:T(8,128)(2,1)S(1)}, bf16[1,127,128]{2,1,0:T(8,128)(2,1)S(1)}, u32[]{:S(2)}, u32[]{:S(2)}) collective-permute-start(bf16[1,127,128]{2,1,0:T(8,128)(2,1)S(1)} %slice.29), channel_id=1, source_target_pairs={{0,2},{2,4},{4,6},{6,8},{8,10},{10,12},{12,14},{1,3},{3,5},{5,7},{... | collective-permute-start | bytes 97544 | tf_op jit(solution)/shard_map/ppermute | solution.py:10
  229.3 1.5 collective-permute-done.1
  230.8 124.3 %while.33 = (s32[]{:T(128)}, f32[1,512,128]{2,1,0:T(8,128)S(1)}, f32[128,128]{1,0:T(8,128)}, bf16[1,639,128]{2,1,0:T(8,128)(2,1)S(1)}, s32[1,639]{1,0:T(1,128)S(...) while((s32[]{:T(128)}, f32[1,512,128]{2,1,0:T(8,128)S(1)}, ...), condition=%wide.region_3.4_spmd.clone, body=%wide.region_2.3_spmd.clone.sunk | while | flops 328711 | bytes 665257 | solution.py:25
  230.9 0.7 fusion.11
  231.9 0.7 fusion.11
  232.8 0.7 fusion.11
  233.8 0.7 fusion.11
  234.8 0.7 fusion.11
  235.8 0.7 fusion.11
  236.7 0.7 fusion.11
  237.7 0.7 fusion.11
  238.7 0.7 fusion.11
  239.6 0.7 fusion.11
  240.6 0.7 fusion.11
  241.6 0.7 fusion.11
  242.6 0.7 fusion.11
  243.5 0.7 fusion.11
  244.5 0.7 fusion.11
  245.5 0.7 fusion.11
  246.4 0.7 fusion.11
  248.4 0.7 fusion.11
  249.4 0.7 fusion.11
  250.3 0.7 fusion.11
  251.3 0.7 fusion.11
  252.3 0.7 fusion.11
  253.2 0.7 fusion.11
  254.2 0.7 fusion.11
  255.2 0.7 fusion.11
  256.2 0.7 fusion.11
  257.1 0.7 fusion.11
  258.1 0.7 fusion.11
  259.1 0.7 fusion.11
  260.0 0.7 fusion.11
  261.0 0.7 fusion.11
  262.0 0.7 fusion.11
  262.9 0.7 fusion.11
  263.9 0.7 fusion.11
  264.9 0.7 fusion.11
  266.8 0.7 fusion.11
  267.8 0.7 fusion.11
  268.8 0.7 fusion.11
  269.7 0.7 fusion.11
  270.7 0.7 fusion.11
  271.7 0.7 fusion.11
  272.7 0.7 fusion.11
  273.6 0.7 fusion.11
  274.6 0.7 fusion.11
  355.1 0.7 multiply_convert_fusion
  (371 shorter events, 93.3 us)
Async XLA Ops:
  6.5 82.2 %all-gather.5.cloned.1.call-start = ((), (), s32[]{:S(2)}) async-start(), calls=%async_computation.1 | async-start | bytes 7077888 | tf_op jit(solution)/shard_map/all_gather | solution.py:34
  8.9 191.0 %all-gather.3.cloned.1.call-start = ((), (), s32[]{:S(2)}) async-start(), calls=%async_computation | async-start | bytes 8650752 | tf_op jit(solution)/shard_map/all_gather | solution.py:37
  199.9 14.5 %copy-start = (s32[1,4096]{1,0:T(1,128)S(1)}, s32[1,4096]{1,0:T(1,128)}, u32[]{:S(2)}) copy-start(s32[1,4096]{1,0:T(1,128)} %param.15) | copy-start | bytes 49156
  209.6 145.5 %copy-start.1 = (f32[128]{0:T(128)S(1)}, f32[128]{0:T(128)}, u32[]{:S(2)}) copy-start(f32[128]{0:T(128)} %param.14) | copy-start | bytes 1540
  209.6 6.1 %collective-permute-start = (bf16[1,6,384]{2,1,0:T(8,128)(2,1)S(1)}, bf16[1,6,384]{2,1,0:T(8,128)(2,1)S(1)}, u32[]{:S(2)}, u32[]{:S(2)}) collective-permute-start(bf16[1,6,384]{2,1,0:T(8,128)(2,1)S(1)} %slice.28), channel_id=1, source_target_pairs={{0,2},{2,4},{4,6},{6,8},{8,10},{10,12},{12,14},{1,3},{3,5},{5,7},{... | collective-permute-start | bytes 13832 | tf_op jit(solution)/shard_map/ppermute | solution.py:10
  223.8 7.0 %collective-permute-start.1 = (bf16[1,127,128]{2,1,0:T(8,128)(2,1)S(1)}, bf16[1,127,128]{2,1,0:T(8,128)(2,1)S(1)}, u32[]{:S(2)}, u32[]{:S(2)}) collective-permute-start(bf16[1,127,128]{2,1,0:T(8,128)(2,1)S(1)} %slice.29), channel_id=1, source_target_pairs={{0,2},{2,4},{4,6},{6,8},{8,10},{10,12},{12,14},{1,3},{3,5},{5,7},{... | collective-permute-start | bytes 97544 | tf_op jit(solution)/shard_map/ppermute | solution.py:10
Sparse Core Ops, SparseCore 0:
  9.4 79.2 all-gather.4
  91.8 108.0 all-gather.2
where the time goes:
time: 367 us; the launch traced here: 363 us
  waiting for transfers between devices  189 us (51%)
  local copies, waits for them, and re-layouts  97 us (26%)
  other arithmetic  35.6 us (10%)
  between operations  13.5 us (4%)
  starting transfers between devices  10.2 us (3%)
  matrix products  9.68 us (3%)
  loops' own time  3.83 us (1%)
    all_gather x1, waiting for transfers between devices, body(): lax.all_gather(block, 'fsdp', axis=2, tiled=True)  111 us
    mul x128, local copies, waits for them, and re-layouts, add_lag(): return total + weight * piece * same  88.5 us
    all_gather x1, waiting for transfers between devices, body(): lax.all_gather(w_in, 'ctx', axis=0, tiled=True).reshape(-1, 3 * channels)  75.4 us
    add x135, other arithmetic, add_lag(): return total + weight * piece * same  24 us
    mul x135, other arithmetic, add_lag(): return total + weight * piece * same  10.7 us
    ppermute x2, starting transfers between devices, passed_along(): lax.ppermute(value, axis, [(source, source + steps) for source in range(l...  10.2 us
    dot_general x1, matrix products, body(): jnp.einsum('bld,dk->blk', lax.all_gather(block, 'fsdp', axis=2, tiled=Tru...  9.68 us
  transfers between devices with their start and end apart: 4, of which 4 were waited for; matrix products, arithmetic and copies ran while one was open for 0% of the time, Pallas kernels for 0%

commit v1 on v0

--- a/solution.py
+++ b/solution.py
@@ -34,7 +34,9 @@
     panel_all = lax.all_gather(w_in, "ctx", axis=0, tiled=True).reshape(-1, 3 * channels)
     summed = jnp.einsum(
         "bld,dk->blk",
-        lax.all_gather(block, "fsdp", axis=2, tiled=True),
+        jnp.concatenate(
+            lax.all_to_all(jnp.stack([block] * lax.axis_size("fsdp")), "fsdp", 0, 0), axis=2
+        ),
         panel_all,
         preferred_element_type=jnp.float32,
     )

time: 367 us -> 386 us (1.052)
  the two profiles are of different devices: /device:TPU:192 before, /device:TPU:222 now
where the time goes in v1:
time: 386 us; the launch traced here: 381 us
  waiting for transfers between devices  196 us (51%)
  local copies, waits for them, and re-layouts  99.4 us (26%)
  other arithmetic  35.6 us (9%)
  starting transfers between devices  21 us (5%)
  between operations  13.5 us (3%)
  matrix products  9.69 us (3%)
    all_to_all x1, waiting for transfers between devices, body(): lax.all_to_all(jnp.stack([block] * lax.axis_size('fsdp')), 'fsdp', 0, 0)  113 us
    mul x128, local copies, waits for them, and re-layouts, add_lag(): return total + weight * piece * same  88.5 us
    all_gather x1, waiting for transfers between devices, body(): lax.all_gather(w_in, 'ctx', axis=0, tiled=True).reshape(-1, 3 * channels)  80.4 us
    add x135, other arithmetic, add_lag(): return total + weight * piece * same  24 us
    ppermute x2, starting transfers between devices, passed_along(): lax.ppermute(value, axis, [(source, source + steps) for source in range(l...  10.9 us
    mul x135, other arithmetic, add_lag(): return total + weight * piece * same  10.7 us
    all_to_all x1, starting transfers between devices, body(): lax.all_to_all(jnp.stack([block] * lax.axis_size('fsdp')), 'fsdp', 0, 0)  10 us
    dot_general x1, matrix products, body(): jnp.einsum('bld,dk->blk', jnp.concatenate(lax.all_to_all(jnp.stack([block...  9.69 us
  transfers between devices with their start and end apart: 4, of which 4 were waited for; matrix products, arithmetic and copies ran while one was open for 0% of the time, Pallas kernels for 0%

profile of v1, /device:TPU:222, one launch (start us, length us, event | category | flops | bytes accessed | tf_op | source)
XLA Modules:
  0.0 381.0 jit_solution(4732949674580800977)
XLA Ops:
  6.5 2.2 all_gather.8
  8.9 4.2 %stack.2 = bf16[32,1,512,256]{2,3,1,0:T(8,128)(2,1)} broadcast(bf16[512,256]{0,1:T(8,128)(2,1)S(1)} %copy.9), dimensions={2,3} | broadcast | bytes 8650752 | tf_op jit(solution)/shard_map/stack | solution.py:38
  13.1 10.0 %all-to-all-start = ((bf16[32,1,512,256]{2,3,1,0:T(8,128)(2,1)}), bf16[32,1,512,256]{2,3,1,0:T(8,128)(2,1)}, u32[]{:S(2)}, u32[]{:S(2)}) async-start(bf16[32,1,512,256]{2,3,1,0:T(8,128)(2,1)} %stack.2), calls=%async_computation | async-start | bytes 16777216 | tf_op jit(solution)/shard_map/all_to_all | solution.py:38
  23.2 1.2 copy.11
  24.5 80.4 %all-gather.2.cloned.1.call-done = bf16[8192,3,128]{0,2,1:T(8,128)(2,1)} async-done(((bf16[1024,3,128]{0,2,1:T(8,128)(2,1)}), bf16[8192,3,128]{0,2,1:T(8,128)(2,1)}) %all-gather.2.cloned.1.call-update) | async-done | bytes 6291472 | tf_op jit(solution)/shard_map/all_gather | solution.py:34
  104.9 112.7 %all-to-all-done = bf16[32,1,512,256]{2,3,1,0:T(8,128)(2,1)} async-done(((bf16[32,1,512,256]{2,3,1,0:T(8,128)(2,1)}), bf16[32,1,512,256]{2,3,1,0:T(8,128)(2,1)}, u32[]{:S(2)}, u32[]{:S(2)}) %all-to-all-start) | async-done | bytes 8388640 | tf_op jit(solution)/shard_map/all_to_all | solution.py:38
  217.6 9.7 %fusion.1 = bf16[1,512,384]{2,1,0:T(8,128)(2,1)S(1)} fusion(bf16[512,8192]{0,1:T(8,128)(2,1)} %bitcast.4, bf16[8192,384]{0,1:T(8,128)(2,1)} %bitcast.26), kind=kOutput, calls=%fused_computation.8 | convolution fusion | flops 3221422080 | bytes 15073280 | tf_op jit(solution)/shard_map/bld,dk->blk/dot_general | solution.py:35
  227.3 5.5 %collective-permute-start = (bf16[1,6,384]{2,1,0:T(8,128)(2,1)S(1)}, bf16[1,6,384]{2,1,0:T(8,128)(2,1)S(1)}, u32[]{:S(2)}, u32[]{:S(2)}) collective-permute-start(bf16[1,6,384]{2,1,0:T(8,128)(2,1)S(1)} %slice.28), channel_id=1, source_target_pairs={{0,2},{2,4},{4,6},{6,8},{8,10},{10,12},{12,14},{1,3},{3,5},{5,7},{... | collective-permute-start | bytes 13832 | tf_op jit(solution)/shard_map/ppermute | solution.py:10
  232.9 1.2 collective-permute-done
  234.2 7.9 %while.32 = (s32[]{:T(128)}, f32[1,512,384]{2,1,0:T(8,128)S(1)}, f32[7,384]{1,0:T(8,128)}, bf16[1,518,384]{2,1,0:T(8,128)(2,1)S(1)}, s32[1,518]{1,0:T(1,128)S(1)...) while((s32[]{:T(128)}, f32[1,512,384]{2,1,0:T(8,128)S(1)}, ...), condition=%wide.region_1.2_spmd.clone, body=%wide.region_0.1_spmd.clone.sunk | while | flops 984071 | bytes 1979049 | solution.py:25
  234.3 0.7 dynamic-slice_reduce_fusion.2
  235.5 0.7 dynamic-slice_reduce_fusion.2
  236.6 0.7 dynamic-slice_reduce_fusion.2
  237.7 0.7 dynamic-slice_reduce_fusion.2
  238.9 0.7 dynamic-slice_reduce_fusion.2
  240.0 0.7 dynamic-slice_reduce_fusion.2
  241.1 0.7 dynamic-slice_reduce_fusion.2
  242.2 5.4 %collective-permute-start.1 = (bf16[1,127,128]{2,1,0:T(8,128)(2,1)S(1)}, bf16[1,127,128]{2,1,0:T(8,128)(2,1)S(1)}, u32[]{:S(2)}, u32[]{:S(2)}) collective-permute-start(bf16[1,127,128]{2,1,0:T(8,128)(2,1)S(1)} %slice.29), channel_id=1, source_target_pairs={{0,2},{2,4},{4,6},{6,8},{8,10},{10,12},{12,14},{1,3},{3,5},{5,7},{... | collective-permute-start | bytes 97544 | tf_op jit(solution)/shard_map/ppermute | solution.py:10
  247.7 1.5 collective-permute-done.1
  249.2 124.2 %while.33 = (s32[]{:T(128)}, f32[1,512,128]{2,1,0:T(8,128)S(1)}, f32[128,128]{1,0:T(8,128)}, bf16[1,639,128]{2,1,0:T(8,128)(2,1)S(1)}, s32[1,639]{1,0:T(1,128)S(...) while((s32[]{:T(128)}, f32[1,512,128]{2,1,0:T(8,128)S(1)}, ...), condition=%wide.region_3.4_spmd.clone, body=%wide.region_2.3_spmd.clone.sunk | while | flops 328711 | bytes 665257 | solution.py:25
  249.3 0.7 fusion.5
  250.3 0.7 fusion.5
  251.3 0.7 fusion.5
  252.3 0.7 fusion.5
  253.2 0.7 fusion.5
  254.2 0.7 fusion.5
  255.2 0.7 fusion.5
  256.1 0.7 fusion.5
  257.1 0.7 fusion.5
  258.1 0.7 fusion.5
  259.0 0.7 fusion.5
  260.0 0.7 fusion.5
  261.0 0.7 fusion.5
  262.0 0.7 fusion.5
  262.9 0.7 fusion.5
  263.9 0.7 fusion.5
  264.9 0.7 fusion.5
  265.8 0.7 fusion.5
  267.8 0.7 fusion.5
  268.8 0.7 fusion.5
  269.7 0.7 fusion.5
  270.7 0.7 fusion.5
  271.7 0.7 fusion.5
  272.6 0.7 fusion.5
  273.6 0.7 fusion.5
  274.6 0.7 fusion.5
  275.5 0.7 fusion.5
  276.5 0.7 fusion.5
  277.5 0.7 fusion.5
  278.5 0.7 fusion.5
  279.4 0.7 fusion.5
  280.4 0.7 fusion.5
  281.4 0.7 fusion.5
  282.3 0.7 fusion.5
  283.3 0.7 fusion.5
  284.3 0.7 fusion.5
  286.2 0.7 fusion.5
  287.2 0.7 fusion.5
  288.2 0.7 fusion.5
  289.1 0.7 fusion.5
  290.1 0.7 fusion.5
  291.1 0.7 fusion.5
  292.0 0.7 fusion.5
  373.5 0.7 multiply_convert_fusion
  (374 shorter events, 94.2 us)
Async XLA Ops:
  13.1 10.1 %copy-start = (bf16[1024,3,128]{2,0,1:T(8,128)(2,1)S(1)}, bf16[1024,3,128]{2,0,1:T(8,128)(2,1)}, u32[]{:S(2)}) copy-start(bf16[1024,3,128]{2,0,1:T(8,128)(2,1)} %param.11) | copy-start | bytes 2359300
  13.1 11.3 %copy-start.1 = (s32[1,4096]{1,0:T(1,128)S(1)}, s32[1,4096]{1,0:T(1,128)}, u32[]{:S(2)}) copy-start(s32[1,4096]{1,0:T(1,128)} %param.15) | copy-start | bytes 49156
  13.1 204.5 %all-to-all-start = ((bf16[32,1,512,256]{2,3,1,0:T(8,128)(2,1)}), bf16[32,1,512,256]{2,3,1,0:T(8,128)(2,1)}, u32[]{:S(2)}, u32[]{:S(2)}) async-start(bf16[32,1,512,256]{2,3,1,0:T(8,128)(2,1)} %stack.2), calls=%async_computation | async-start | bytes 16777216 | tf_op jit(solution)/shard_map/all_to_all | solution.py:38
  23.1 81.8 %all-gather.2.cloned.1.call-start = ((), (), s32[]{:S(2)}) async-start(), calls=%async_computation.1 | async-start | bytes 7077888 | tf_op jit(solution)/shard_map/all_gather | solution.py:34
  227.3 146.2 %copy-start.2 = (f32[128]{0:T(128)S(1)}, f32[128]{0:T(128)}, u32[]{:S(2)}) copy-start(f32[128]{0:T(128)} %param.14) | copy-start | bytes 1540
  227.3 6.8 %collective-permute-start = (bf16[1,6,384]{2,1,0:T(8,128)(2,1)S(1)}, bf16[1,6,384]{2,1,0:T(8,128)(2,1)S(1)}, u32[]{:S(2)}, u32[]{:S(2)}) collective-permute-start(bf16[1,6,384]{2,1,0:T(8,128)(2,1)S(1)} %slice.28), channel_id=1, source_target_pairs={{0,2},{2,4},{4,6},{6,8},{8,10},{10,12},{12,14},{1,3},{3,5},{5,7},{... | collective-permute-start | bytes 13832 | tf_op jit(solution)/shard_map/ppermute | solution.py:10
  242.2 7.0 %collective-permute-start.1 = (bf16[1,127,128]{2,1,0:T(8,128)(2,1)S(1)}, bf16[1,127,128]{2,1,0:T(8,128)(2,1)S(1)}, u32[]{:S(2)}, u32[]{:S(2)}) collective-permute-start(bf16[1,127,128]{2,1,0:T(8,128)(2,1)S(1)} %slice.29), channel_id=1, source_target_pairs={{0,2},{2,4},{4,6},{6,8},{8,10},{10,12},{12,14},{1,3},{3,5},{5,7},{... | collective-permute-start | bytes 97544 | tf_op jit(solution)/shard_map/ppermute | solution.py:10
Sparse Core Ops, SparseCore 0:
  26.0 78.8 all-gather.1
